TPU v7x, 32 devices: a whole 2x2x4 slice. The times are simulated.
32 devices in a mesh: ax: 8 (over z, y), az: 2 (over x), rad: 2 (over core).
Axes of the slice: x: 2, y: 2, z: 4, core: 2. Of those that a mesh axis runs over, the one named last changes fastest.
Arguments:
- state: float32 [5, 64, 128, 1024], P(None, 'ax', 'rad', 'az'), may hold values from -6 to 6
- section: float32 [5, 64, 128, 1024], P(None, 'ax', 'rad', 'az'), may hold values from -6 to 6
- mean_axial: float32 [128], P('rad'), may hold values from 0.3 to 0.6
- mean_swirl: float32 [128], P('rad'), may hold values from 0.1 to 0.4
- mean_density: float32 [128], P('rad'), may hold values from 0.8 to 1.25
- sound_squared: float32 [128], P('rad'), may hold values from 0.8 to 1.25
Outputs:
- new_state: float32 [5, 64, 128, 1024], P(None, 'ax', 'rad', 'az')
- new_section: float32 [5, 64, 128, 1024], P(None, 'ax', 'rad', 'az')
All inputs are finite; a program needn't handle non-finite values.
Results may differ from a plain program's by a relative error of at most 0.00005.
Values sent between devices are 32-bit elements; how exact they have to be, the bound alone decides.
A program may use at most 128 MiB of HBM per device.

v0:
```python
import functools
import math

import jax
import jax.numpy as jnp
import numpy as np
from jax import lax
from jax.experimental import pallas as pl
from jax.experimental.pallas import tpu as pltpu
from jax.sharding import PartitionSpec as P

NT = 1024
MESH = pl.DeviceIdType.MESH

drp_coeffs = (0.770882380518, -0.166705904415, 0.02084314277)
section_keep = -0.4178904745
section_gain = 0.3792103129999
time_step = 0.25
HALO = 3
RIM = 8


def spectral_tables(owners, local):
    s = np.arange(local)[:, None]
    t = np.arange(local)[None, :]
    tables = []
    for d in range(owners):
        spacing = (t - s + d * local) % NT
        spacing = np.where(spacing > NT // 2, spacing - NT, spacing)
        angle = np.pi * spacing / NT
        safe = np.where(spacing == 0, 1.0, np.sin(angle))
        parity = 1.0 - 2.0 * (spacing % 2)
        tables.append(np.where(spacing == 0, 0.0, 0.5 * parity * np.cos(angle) / safe))
    full = np.stack(tables).astype(np.float32)
    high = full.astype(jnp.bfloat16)
    low = (full - high.astype(np.float32)).astype(jnp.bfloat16)
    return np.stack([high, low], axis=1)


def azimuthal(values, high_table, low_table):
    fields, rows, local = values.shape
    flat = values.reshape(fields * rows, local)
    high = flat.astype(jnp.bfloat16)
    low = (flat - high.astype(jnp.float32)).astype(jnp.bfloat16)
    dot = functools.partial(jnp.dot, preferred_element_type=jnp.float32)
    g = dot(high, high_table) + dot(low, high_table) + dot(high, low_table)
    return g.reshape(fields, rows, local)


def add_azimuthal(ns, coef, c, g):
    rate = coef[1]
    ns[0, c] += rate * g[0] + coef[5] * g[3]
    ns[1, c] += rate * g[1]
    ns[2, c] += rate * g[2]
    ns[3, c] += rate * g[3] + coef[7] * g[4]
    ns[4, c] += rate * g[4] + coef[6] * g[3]


def kernel(
    sizes, state, section, axial_speed, swirl, density_in, sound, table_in, ns, nst, late, coef,
    st, pr, other, table, means,
    load_sem, az_send, az_recv, ax_send, ax_recv, rad_send, rad_recv,
):
    n_ax, n_az, n_rad, count, rows, local = sizes
    ax = lax.axis_index("ax")
    az = lax.axis_index("az")
    rad = lax.axis_index("rad")
    has_prev, has_next = ax > 0, ax < n_ax - 1
    has_low, has_high = rad > 0, rad < n_rad - 1

    def az_copy(d, c, last=False):
        return pltpu.make_async_remote_copy(
            src_ref=state.at[:, c],
            dst_ref=late.at[d - 1] if last else other.at[d - 1, :, c],
            send_sem=az_send.at[d - 1, c],
            recv_sem=az_recv.at[d - 1, c],
            device_id={"az": lax.rem(az + d, n_az)},
            device_id_type=MESH,
        )

    def ax_copy(up):
        return pltpu.make_async_remote_copy(
            src_ref=state.at[:, pl.ds(count - HALO if up else 0, HALO)],
            dst_ref=st.at[:, pl.ds(0 if up else count + HALO, HALO)],
            send_sem=ax_send.at[0 if up else 1],
            recv_sem=ax_recv.at[0 if up else 1],
            device_id={"ax": ax + 1 if up else ax - 1},
            device_id_type=MESH,
        )

    def rad_copy(up, k):
        return pltpu.make_async_remote_copy(
            src_ref=state.at[2 + 2 * k, :, pl.ds(rows - RIM if up else 0, RIM)],
            dst_ref=pr.at[k, :, pl.ds(0 if up else rows + RIM, RIM)],
            send_sem=rad_send.at[0 if up else 1, k],
            recv_sem=rad_recv.at[0 if up else 1, k],
            device_id={"rad": rad + 1 if up else rad - 1},
            device_id_type=MESH,
        )

    loads = [
        pltpu.make_async_copy(state, st.at[:, pl.ds(HALO, count)], load_sem.at[0]),
        pltpu.make_async_copy(section, ns, load_sem.at[1]),
        pltpu.make_async_copy(state.at[2], pr.at[0, :, pl.ds(RIM, rows)], load_sem.at[2]),
        pltpu.make_async_copy(state.at[4], pr.at[1, :, pl.ds(RIM, rows)], load_sem.at[3]),
        pltpu.make_async_copy(table_in, table, load_sem.at[4]),
    ]
    vectors = [
        pltpu.make_async_copy(ref, means.at[i], load_sem.at[5 + i])
        for i, ref in enumerate((axial_speed, swirl, density_in, sound))
    ]

    barrier = pltpu.get_barrier_semaphore()

    def greet(axis, index):
        pl.semaphore_signal(barrier, inc=1, device_id={axis: index}, device_id_type=MESH)

    pl.when(has_prev)(lambda: greet("ax", ax - 1))
    pl.when(has_next)(lambda: greet("ax", ax + 1))
    for d in range(1, n_az):
        greet("az", lax.rem(az + d, n_az))
    pl.when(has_low)(lambda: greet("rad", rad - 1))
    pl.when(has_high)(lambda: greet("rad", rad + 1))
    for copy in vectors:
        copy.start()
    met = n_az - 1
    for there in (has_prev, has_next, has_low, has_high):
        met = met + there.astype(jnp.int32)
    pl.semaphore_wait(barrier, met)

    def send_plane(c, carry):
        for d in range(1, n_az):
            az_copy(d, c).start()
        return carry

    send_plane(0, 0)
    pl.when(has_next)(lambda: ax_copy(True).start())
    pl.when(has_prev)(lambda: ax_copy(False).start())
    for k in range(2):
        pl.when(has_high)(lambda: rad_copy(True, k).start())
        pl.when(has_low)(lambda: rad_copy(False, k).start())
    lax.fori_loop(1, count - 1, send_plane, 0)
    for d in range(1, n_az):
        az_copy(d, count - 1, True).start()
    for copy in loads:
        copy.start()

    for copy in vectors:
        copy.wait()

    pick = lax.broadcasted_iota(jnp.int32, (rows, rows), 0) == lax.broadcasted_iota(
        jnp.int32, (rows, rows), 1
    )

    def column(i):
        line = jnp.broadcast_to(means[i], (rows, rows))
        return jnp.sum(jnp.where(pick, line, 0.0), axis=1, keepdims=True)

    cell = lax.broadcasted_iota(jnp.int32, (rows, local), 0) + rad * rows
    inv_radius = 1.0 / (NT / (2.0 * math.pi) + cell.astype(jnp.float32) + 0.5)
    density = jnp.broadcast_to(column(2), (rows, local))
    minus = -time_step
    inverse = minus / density
    stiff = minus * density * column(3)
    coef[0] = jnp.broadcast_to(minus * column(0), (rows, local))
    coef[1] = minus * column(1) * inv_radius
    coef[2] = minus * density
    coef[3] = stiff
    coef[4] = inverse
    coef[5] = minus * density * inv_radius
    coef[6] = stiff * inv_radius
    coef[7] = inverse * inv_radius

    def radial(k, c):
        total = jnp.zeros((rows, local), jnp.float32)
        for j in range(1, 4):
            total += drp_coeffs[j - 1] * (
                pr[k, c, pl.ds(RIM + j, rows)] - pr[k, c, pl.ds(RIM - j, rows)]
            )
        return total

    def axial(f, c):
        total = jnp.zeros((rows, local), jnp.float32)
        for j in range(1, 4):
            total += drp_coeffs[j - 1] * (st[f, c + HALO + j] - st[f, c + HALO - j])
        return total

    for copy in loads:
        copy.wait()

    def wall(low):
        def fill(c, carry):
            for k, sign in enumerate((-1.0, 1.0)):
                for j in range(3):
                    if low:
                        pr[k, c, pl.ds(RIM - 1 - j, 1)] = sign * pr[k, c, pl.ds(RIM + j, 1)]
                    else:
                        pr[k, c, pl.ds(RIM + rows + j, 1)] = sign * pr[
                            k, c, pl.ds(RIM + rows - 1 - j, 1)
                        ]
            return carry

        lax.fori_loop(0, count, fill, 0)

    pl.when(jnp.logical_not(has_low))(lambda: wall(True))
    pl.when(jnp.logical_not(has_high))(lambda: wall(False))
    for k in range(2):
        pl.when(has_low)(lambda: rad_copy(True, k).wait_recv())
        pl.when(has_high)(lambda: rad_copy(False, k).wait_recv())

    def own_part(c, carry):
        for f in range(5):
            ns[f, c] = section_keep * ns[f, c]
        spread = radial(0, c)
        ns[0, c] += coef[2] * spread
        ns[4, c] += coef[3] * spread
        ns[2, c] += coef[4] * radial(1, c)
        add_azimuthal(ns, coef, c, azimuthal(st[:, HALO + c], table[0, 0], table[0, 1]))
        return carry

    lax.fori_loop(0, count, own_part, 0)

    def far_part(c, carry):
        def step(d, inner):
            az_copy(d, c).wait_recv()
            add_azimuthal(ns, coef, c, azimuthal(other[d - 1, :, c], table[d, 0], table[d, 1]))
            return inner

        return lax.fori_loop(1, n_az, step, carry)

    def axial_part(c, carry):
        along = axial(1, c)
        press = axial(4, c)
        speed = coef[0]
        ns[0, c] += speed * axial(0, c) + coef[2] * along
        ns[1, c] += speed * along + coef[4] * press
        ns[2, c] += speed * axial(2, c)
        ns[3, c] += speed * axial(3, c)
        ns[4, c] += speed * press + coef[3] * along
        return carry

    def finish(c, carry):
        for f in range(5):
            nst[f, c] = st[f, HALO + c] + section_gain * ns[f, c]
        return carry

    early = count - 2
    lax.fori_loop(0, early, far_part, 0)

    def clear(start):
        st[:, pl.ds(start, HALO)] = jnp.zeros((5, HALO, rows, local), jnp.float32)

    pl.when(has_prev)(lambda: ax_copy(True).wait_recv())
    pl.when(has_next)(lambda: ax_copy(False).wait_recv())
    pl.when(jnp.logical_not(has_prev))(lambda: clear(0))
    pl.when(jnp.logical_not(has_next))(lambda: clear(count + HALO))
    lax.fori_loop(0, count, axial_part, 0)
    lax.fori_loop(0, early, finish, 0)
    lax.fori_loop(early, count - 1, lambda c, carry: finish(c, far_part(c, carry)), 0)
    for f in range(5):
        nst[f, count - 1] = st[f, HALO + count - 1]

    def drain(c, carry):
        for d in range(1, n_az):
            az_copy(d, c).wait_send()
        return carry

    lax.fori_loop(0, count - 1, drain, 0)
    pl.when(has_next)(lambda: ax_copy(True).wait_send())
    pl.when(has_prev)(lambda: ax_copy(False).wait_send())
    for k in range(2):
        pl.when(has_high)(lambda: rad_copy(True, k).wait_send())
        pl.when(has_low)(lambda: rad_copy(False, k).wait_send())
    for d in range(1, n_az):
        az_copy(d, count - 1, True).wait_send()
        az_copy(d, count - 1, True).wait_recv()


def write_kernel(n_az, ns, nst, late, coef, table, out_state, out_section, fin, sem):
    last = ns.shape[1] - 1

    def copies(c):
        return (
            pltpu.make_async_copy(ns.at[:, c], out_section.at[:, c], sem.at[0, c]),
            pltpu.make_async_copy(nst.at[:, c], out_state.at[:, c], sem.at[1, c]),
        )

    def begin(c, carry):
        for copy in copies(c):
            copy.start()
        return carry

    def end(c, carry):
        for copy in copies(c):
            copy.wait()
        return carry

    lax.fori_loop(0, last, begin, 0)

    fin[:, 0] = ns[:, last]

    def far_part(d, carry):
        add_azimuthal(fin, coef, 0, azimuthal(late[d - 1], table[d, 0], table[d, 1]))
        return carry

    lax.fori_loop(1, n_az, far_part, 0)
    for f in range(5):
        fin[f, 1] = nst[f, last] + section_gain * fin[f, 0]
    ends = (
        pltpu.make_async_copy(fin.at[:, 0], out_section.at[:, last], sem.at[0, last]),
        pltpu.make_async_copy(fin.at[:, 1], out_state.at[:, last], sem.at[1, last]),
    )
    for copy in ends:
        copy.start()
    lax.fori_loop(0, last, end, 0)
    for copy in ends:
        copy.wait()


def body(mesh_sizes, state, section, mean_axial, mean_swirl, mean_density, sound_squared):
    n_ax, n_az, n_rad = mesh_sizes
    _, count, rows, local = state.shape
    table = jnp.asarray(spectral_tables(n_az, local))
    whole = (5, count, rows, local)
    late = (n_az - 1, 5, rows, local)
    coef = (8, rows, local)
    far = pl.BlockSpec(memory_space=pltpu.HBM)
    near = pl.BlockSpec(memory_space=pltpu.VMEM)
    f32 = jnp.float32
    dma = pltpu.SemaphoreType.DMA
    pin = functools.partial(pltpu.with_memory_space_constraint, memory_space=pltpu.HBM)
    ns, nst, late, coef = pl.pallas_call(
        functools.partial(kernel, (n_ax, n_az, n_rad, count, rows, local)),
        out_shape=tuple(pltpu.VMEM(shape, f32) for shape in (whole, whole, late, coef)),
        in_specs=[far] * 7,
        out_specs=(near,) * 4,
        scratch_shapes=[
            pltpu.VMEM((5, count + 2 * HALO, rows, local), f32),
            pltpu.VMEM((2, count, rows + 2 * RIM, local), f32),
            pltpu.VMEM((n_az - 1, 5, count - 1, rows, local), f32),
            pltpu.VMEM((n_az, 2, local, local), jnp.bfloat16),
            pltpu.VMEM((4, 1, rows), f32),
            dma((9,)),
            dma((n_az - 1, count)),
            dma((n_az - 1, count)),
            dma((2,)),
            dma((2,)),
            dma((2, 2)),
            dma((2, 2)),
        ],
        compiler_params=pltpu.CompilerParams(
            collective_id=0, has_side_effects=True, vmem_limit_bytes=28 * 2**20
        ),
        cost_estimate=pl.CostEstimate(
            flops=6 * 5 * count * rows * local * NT,
            bytes_accessed=4 * 4 * 5 * count * rows * local,
            transcendentals=0,
        ),
    )(
        pin(state),
        pin(section),
        pin(mean_axial[None]),
        pin(mean_swirl[None]),
        pin(mean_density[None]),
        pin(sound_squared[None]),
        pin(table),
    )
    return pl.pallas_call(
        functools.partial(write_kernel, n_az),
        out_shape=(jax.ShapeDtypeStruct(whole, f32), jax.ShapeDtypeStruct(whole, f32)),
        in_specs=[near] * 5,
        out_specs=(far, far),
        scratch_shapes=[pltpu.VMEM((5, 2, rows, local), f32), dma((2, count))],
        compiler_params=pltpu.CompilerParams(vmem_limit_bytes=8 * 2**20),
    )(ns, nst, late, coef, table)


def solution(mesh):
    spec = P(None, "ax", "rad", "az")
    sizes = (mesh.shape["ax"], mesh.shape["az"], mesh.shape["rad"])
    return jax.shard_map(
        functools.partial(body, sizes),
        mesh=mesh,
        in_specs=(spec, spec, P("rad"), P("rad"), P("rad"), P("rad")),
        out_specs=(spec, spec),
        check_vma=False,
    )
```

profile of v0, /device:TPU:0, one launch (start us, length us, event | category | flops | bytes accessed | tf_op | source)
XLA Modules:
  0.0 122.5 jit_solution(2904303137650100781)
XLA Ops:
  0.6 0.0 copy-start
  0.6 117.8 %shard_map.86 = (f32[5,8,64,512]{3,2,1,0:T(8,128)S(1)}, f32[5,8,64,512]{3,2,1,0:T(8,128)S(1)}, f32[1,5,64,512]{3,2,1,0:T(8,128)S(1)}, f32[8,64,512]{2,1,0:T(8,128)S(1)}) custom-call(f32[5,8,64,512]{3,2,1,0:T(8,128)} %state.1, f32[5,8,64,512]{3,2,1,0:T(8,128)} %section.1, f32[1,64]{1,0:T(1,128)} %bitcast.4, f32[1,64]{1,0:T(1,128)} %bitcast.5, ...), custom_call_target="tpu_custom_call" | custom-call | flops 8053063680 | bytes 20971520 | tf_op jit(solution)/shard_map/pallas_call | solution.py:332
  118.4 0.0 copy-done
  118.4 4.1 %shard_map.87 = (f32[5,8,64,512]{3,2,1,0:T(8,128)}, f32[5,8,64,512]{3,2,1,0:T(8,128)}) custom-call(f32[5,8,64,512]{3,2,1,0:T(8,128)S(1)} %get-tuple-element.6.ns, f32[5,8,64,512]{3,2,1,0:T(8,128)S(1)} %get-tuple-element.7.nst, f32[1,5,64,512]{3,2,1,0:T(8,128)S(1)} %get-tuple-element.8.late, f32[8,64,512]{2,1,0:T(8,128)S(1)} %get-tuple-element.9.coef, ...), custom_call_target="tpu_custom_call" | custom-call | tf_op jit(solution)/shard_map/pallas_call | solution.py:368
Async XLA Ops:
  0.6 117.8 %copy-start = (bf16[2,2,512,512]{3,2,1,0:T(8,128)(2,1)S(1)}, bf16[2,2,512,512]{3,2,1,0:T(8,128)(2,1)}, u32[]{:S(2)}) copy-start(bf16[2,2,512,512]{3,2,1,0:T(8,128)(2,1)} %constant.2.clone.table_in.table) | copy-start | bytes 6291460
where the time goes:
time: 123 us
  Pallas kernels  122 us (99%)
    pallas_call x1, Pallas kernels, body(): pl.pallas_call(functools.partial(kernel, (n_ax, n_az, n_rad, count, rows,...  118 us
    pallas_call x1, Pallas kernels, body(): pl.pallas_call(functools.partial(write_kernel, n_az), out_shape=(jax.Shap...  4.07 us

commit v1 on v0

v1 whole, which is shorter than its diff:
```python
import functools
import math

import jax
import jax.numpy as jnp
import numpy as np
from jax import lax
from jax.experimental import pallas as pl
from jax.experimental.pallas import tpu as pltpu
from jax.sharding import PartitionSpec as P

NT = 1024
MESH = pl.DeviceIdType.MESH

drp_coeffs = (0.770882380518, -0.166705904415, 0.02084314277)
section_keep = -0.4178904745
section_gain = 0.3792103129999
time_step = 0.25
HALO = 3
RIM = 8
CUTS = 4
NODES = 64
WIDTH = 2 * NODES


def split(full):
    full = full.astype(np.float32)
    high = full.astype(jnp.bfloat16)
    low = (full - high.astype(np.float32)).astype(jnp.bfloat16)
    return np.stack([high, low])


def near_table(local):
    s = np.arange(local)[:, None]
    t = np.arange(local)[None, :]
    spacing = t - s
    angle = np.pi * spacing / NT
    safe = np.where(spacing == 0, 1.0, np.sin(angle))
    parity = 1.0 - 2.0 * (spacing % 2)
    return split(np.where(spacing == 0, 0.0, 0.5 * parity * np.cos(angle) / safe))


def quadrature():
    step = 0.16
    u = (np.arange(NODES) + 0.5) * step
    scale = 2.0 * np.pi / NT
    t = scale * np.sinh(u)
    weight = step * scale * np.cosh(u) * (NT / np.pi) / -np.expm1(-NT * t)
    return t, weight


def far_tables(owners, local):
    t, weight = quadrature()
    k = np.arange(local)[:, None]
    sign = 1.0 - 2.0 * (k % 2)
    into = np.concatenate([sign * np.exp(-k * t), sign * np.exp(-(local - 1 - k) * t)], axis=1)
    t, weight = t[:, None], weight[:, None]
    j = np.arange(local)[None, :]
    sign = 1.0 - 2.0 * (j % 2)
    outof = []
    for d in range(1, owners):
        below = -0.5 * sign * weight * np.exp(-(NT - d * local - j) * t)
        above = 0.5 * sign * weight * np.exp(-(d * local + j - local + 1) * t)
        outof.append(split(np.concatenate([below, above], axis=0)))
    return split(into), np.stack(outof)


def product(values, high_table, low_table):
    high = values.astype(jnp.bfloat16)
    low = (values - high.astype(jnp.float32)).astype(jnp.bfloat16)
    dot = functools.partial(jnp.dot, preferred_element_type=jnp.float32)
    return dot(high, high_table) + dot(low, high_table) + dot(high, low_table)


def kernel(
    sizes, state, section, axial_speed, swirl, density_in, sound, near_in, into_in, outof_in, ns, nst,
    st, pr, halo, relay, sums, other, near, into, outof, coef, means,
    load_sem, az_send, az_recv, ax_send, ax_recv, hop_send, hop_recv, pass_send, rad_send, rad_recv,
):
    n_ax, n_az, n_rad, count, rows, local = sizes
    cut = rows // CUTS
    ax = lax.axis_index("ax")
    az = lax.axis_index("az")
    rad = lax.axis_index("rad")
    has_prev, has_next = ax > 0, ax < n_ax - 1
    has_low, has_high = rad > 0, rad < n_rad - 1

    levels = n_ax // 2 if n_ax % 2 == 0 and n_ax <= 2 * CUTS else 0
    level = lax.div(ax, 2)
    odd = lax.rem(ax, 2) == 1
    even = jnp.logical_not(odd)
    zero = jnp.int32(0)
    if levels:
        rest = lax.div((levels - 1 - level) * CUTS, levels)
        gone = lax.div(level * CUTS, levels)
        hop_up = jnp.where(jnp.logical_and(odd, has_next), rest, zero)
        hop_down = jnp.where(jnp.logical_and(even, has_prev), gone, zero)
        pass_up = jnp.where(jnp.logical_and(even, ax + 2 < n_ax), rest, zero)
        pass_down = jnp.where(jnp.logical_and(odd, ax >= 3), gone, zero)
    else:
        hop_up = hop_down = pass_up = pass_down = zero
    hops = range(CUTS - 1 if levels else 0)

    def az_copy(d, c):
        return pltpu.make_async_remote_copy(
            src_ref=sums.at[:, c],
            dst_ref=other.at[d - 1, :, c],
            send_sem=az_send.at[d - 1, c],
            recv_sem=az_recv.at[d - 1, c],
            device_id={"az": lax.rem(az + d, n_az)},
            device_id_type=MESH,
        )

    def edge(up, q):
        return state.at[:, pl.ds(count - HALO if up else 0, HALO), pl.ds(q * cut, cut)]

    def landing(up, q):
        return halo.at[0 if up else 1, :, :, pl.ds(q * cut, cut)]

    def ax_copy(up, q):
        way = 0 if up else 1
        return pltpu.make_async_remote_copy(
            src_ref=edge(up, q),
            dst_ref=landing(up, q),
            send_sem=ax_send.at[way, q],
            recv_sem=ax_recv.at[way, q],
            device_id={"ax": ax + 1 if up else ax - 1},
            device_id_type=MESH,
        )

    def hop_copy(up, q):
        return pltpu.make_async_remote_copy(
            src_ref=edge(up, q),
            dst_ref=relay.at[q],
            send_sem=hop_send.at[q],
            recv_sem=hop_recv.at[q],
            device_id={"ax": ax - 1 if up else ax + 1},
            device_id_type=MESH,
        )

    def pass_copy(up, q):
        return pltpu.make_async_remote_copy(
            src_ref=relay.at[q],
            dst_ref=landing(up, q),
            send_sem=pass_send.at[q],
            recv_sem=ax_recv.at[0 if up else 1, q],
            device_id={"ax": ax + 2 if up else ax - 2},
            device_id_type=MESH,
        )

    def rad_copy(up, k):
        return pltpu.make_async_remote_copy(
            src_ref=state.at[2 + 2 * k, :, pl.ds(rows - RIM if up else 0, RIM)],
            dst_ref=pr.at[k, :, pl.ds(0 if up else rows + RIM, RIM)],
            send_sem=rad_send.at[0 if up else 1, k],
            recv_sem=rad_recv.at[0 if up else 1, k],
            device_id={"rad": rad + 1 if up else rad - 1},
            device_id_type=MESH,
        )

    loads = [
        pltpu.make_async_copy(state, st.at[:, pl.ds(HALO, count)], load_sem.at[0]),
        pltpu.make_async_copy(into_in, into, load_sem.at[1]),
        pltpu.make_async_copy(section, ns, load_sem.at[2]),
        pltpu.make_async_copy(state.at[2], pr.at[0, :, pl.ds(RIM, rows)], load_sem.at[3]),
        pltpu.make_async_copy(state.at[4], pr.at[1, :, pl.ds(RIM, rows)], load_sem.at[4]),
        pltpu.make_async_copy(near_in, near, load_sem.at[5]),
        pltpu.make_async_copy(outof_in, outof, load_sem.at[6]),
    ]
    vectors = [
        pltpu.make_async_copy(ref, means.at[i], load_sem.at[7 + i])
        for i, ref in enumerate((axial_speed, swirl, density_in, sound))
    ]

    barrier = pltpu.get_barrier_semaphore()

    def greet(axis, index):
        pl.semaphore_signal(barrier, inc=1, device_id={axis: index}, device_id_type=MESH)

    met = zero + (n_az - 1)
    for d in (-2, -1, 1, 2) if levels else (-1, 1):
        there = jnp.logical_and(ax + d >= 0, ax + d < n_ax)
        pl.when(there)(lambda: greet("ax", ax + d))
        met = met + there.astype(jnp.int32)
    for d in range(1, n_az):
        greet("az", lax.rem(az + d, n_az))
    pl.when(has_low)(lambda: greet("rad", rad - 1))
    pl.when(has_high)(lambda: greet("rad", rad + 1))
    met = met + has_low.astype(jnp.int32) + has_high.astype(jnp.int32)
    for copy in vectors + loads:
        copy.start()
    pl.semaphore_wait(barrier, met)

    up_direct = lambda q: jnp.logical_and(has_next, q >= hop_up)
    down_direct = lambda q: jnp.logical_and(has_prev, q >= hop_down)

    def send(q, first):
        up = jnp.logical_and(up_direct(q), odd if first else even)
        down = jnp.logical_and(down_direct(q), even if first else odd)
        pl.when(up)(lambda: ax_copy(True, q).start())
        pl.when(down)(lambda: ax_copy(False, q).start())

    for q in hops:
        pl.when(q < hop_up)(lambda: hop_copy(True, q).start())
        pl.when(q < hop_down)(lambda: hop_copy(False, q).start())
    for first in (True, False):
        for q in range(CUTS):
            send(q, first)
    for k in range(2):
        pl.when(has_high)(lambda: rad_copy(True, k).start())
        pl.when(has_low)(lambda: rad_copy(False, k).start())

    for copy in vectors:
        copy.wait()

    pick = lax.broadcasted_iota(jnp.int32, (rows, rows), 0) == lax.broadcasted_iota(
        jnp.int32, (rows, rows), 1
    )

    def column(i):
        line = jnp.broadcast_to(means[i], (rows, rows))
        return jnp.sum(jnp.where(pick, line, 0.0), axis=1, keepdims=True)

    cell = lax.broadcasted_iota(jnp.int32, (rows, local), 0) + rad * rows
    inv_radius = 1.0 / (NT / (2.0 * math.pi) + cell.astype(jnp.float32) + 0.5)
    density = jnp.broadcast_to(column(2), (rows, local))
    minus = -time_step
    inverse = minus / density
    stiff = minus * density * column(3)
    coef[0] = jnp.broadcast_to(minus * column(0), (rows, local))
    coef[1] = minus * column(1) * inv_radius
    coef[2] = minus * density
    coef[3] = stiff
    coef[4] = inverse
    coef[5] = minus * density * inv_radius
    coef[6] = stiff * inv_radius
    coef[7] = inverse * inv_radius

    for copy in loads[:2]:
        copy.wait()

    def gather(c, carry):
        flat = st[:, HALO + c].reshape(5 * rows, local)
        sums[:, c] = product(flat, into[0], into[1]).reshape(5, rows, WIDTH)
        for d in range(1, n_az):
            az_copy(d, c).start()
        return carry

    lax.fori_loop(0, count, gather, 0)

    for start in (0, count + HALO):
        st[:, pl.ds(start, HALO)] = jnp.zeros((5, HALO, rows, local), jnp.float32)

    for copy in loads[2:]:
        copy.wait()

    def wall(low):
        def fill(c, carry):
            for k, sign in enumerate((-1.0, 1.0)):
                for j in range(3):
                    if low:
                        pr[k, c, pl.ds(RIM - 1 - j, 1)] = sign * pr[k, c, pl.ds(RIM + j, 1)]
                    else:
                        pr[k, c, pl.ds(RIM + rows + j, 1)] = sign * pr[
                            k, c, pl.ds(RIM + rows - 1 - j, 1)
                        ]
            return carry

        lax.fori_loop(0, count, fill, 0)

    pl.when(jnp.logical_not(has_low))(lambda: wall(True))
    pl.when(jnp.logical_not(has_high))(lambda: wall(False))
    for k in range(2):
        pl.when(has_low)(lambda: rad_copy(True, k).wait_recv())
        pl.when(has_high)(lambda: rad_copy(False, k).wait_recv())

    def radial(k, c):
        total = jnp.zeros((rows, local), jnp.float32)
        for j in range(1, 4):
            total += drp_coeffs[j - 1] * (
                pr[k, c, pl.ds(RIM + j, rows)] - pr[k, c, pl.ds(RIM - j, rows)]
            )
        return total

    def axial(f, c):
        total = jnp.zeros((rows, local), jnp.float32)
        for j in range(1, 4):
            total += drp_coeffs[j - 1] * (st[f, c + HALO + j] - st[f, c + HALO - j])
        return total

    def pass_on(q):
        @pl.when(q < pass_up)
        def _():
            hop_copy(True, q).wait_recv()
            pass_copy(True, q).start()

        @pl.when(q < pass_down)
        def _():
            hop_copy(False, q).wait_recv()
            pass_copy(False, q).start()

    def plane(c, carry):
        spread = radial(0, c)
        along = axial(1, c)
        press = axial(4, c)
        speed = coef[0]
        ns[0, c] = section_keep * ns[0, c] + speed * axial(0, c) + coef[2] * (along + spread)
        ns[1, c] = section_keep * ns[1, c] + speed * along + coef[4] * press
        ns[2, c] = section_keep * ns[2, c] + speed * axial(2, c) + coef[4] * radial(1, c)
        ns[3, c] = section_keep * ns[3, c] + speed * axial(3, c)
        ns[4, c] = section_keep * ns[4, c] + speed * press + coef[3] * (along + spread)
        g = product(st[:, HALO + c].reshape(5 * rows, local), near[0], near[1])
        for d in range(1, n_az):
            az_copy(d, c).wait_recv()
            g += product(other[d - 1, :, c].reshape(5 * rows, WIDTH), outof[d - 1, 0], outof[d - 1, 1])
        g = g.reshape(5, rows, local)
        rate = coef[1]
        ns[0, c] += rate * g[0] + coef[5] * g[3]
        ns[1, c] += rate * g[1]
        ns[2, c] += rate * g[2]
        ns[3, c] += rate * g[3] + coef[7] * g[4]
        ns[4, c] += rate * g[4] + coef[6] * g[3]
        for f in range(5):
            nst[f, c] = st[f, HALO + c] + section_gain * ns[f, c]
        for q in hops:
            pl.when(c == min(2 * q + 1, count - 1))(lambda: pass_on(q))
        return carry

    lax.fori_loop(0, count, plane, 0)

    def rim(up, q):
        way = 0 if up else 1
        lines = pl.ds(q * cut, cut)
        speed, dense, stiff, inverse = coef[0, lines], coef[2, lines], coef[3, lines], coef[4, lines]
        for reach in range(HALO):
            p = reach if up else count - 1 - reach
            grads = []
            for f in range(5):
                total = jnp.zeros((cut, local), jnp.float32)
                for j in range(reach + 1, HALO + 1):
                    past = j - reach - 1
                    total += drp_coeffs[j - 1] * halo[way, f, HALO - 1 - past if up else past, lines]
                grads.append(-total if up else total)
            more = (
                speed * grads[0] + dense * grads[1],
                speed * grads[1] + inverse * grads[4],
                speed * grads[2],
                speed * grads[3],
                speed * grads[4] + stiff * grads[1],
            )
            for f in range(5):
                value = ns[f, p, lines] + more[f]
                ns[f, p, lines] = value
                nst[f, p, lines] = st[f, HALO + p, lines] + section_gain * value

    for q in range(CUTS):
        @pl.when(has_prev)
        def _():
            ax_copy(True, q).wait_recv()
            rim(True, q)

        @pl.when(has_next)
        def _():
            ax_copy(False, q).wait_recv()
            rim(False, q)

    def drain(c, carry):
        for d in range(1, n_az):
            az_copy(d, c).wait_send()
        return carry

    lax.fori_loop(0, count, drain, 0)
    for q in range(CUTS):
        pl.when(up_direct(q))(lambda: ax_copy(True, q).wait_send())
        pl.when(down_direct(q))(lambda: ax_copy(False, q).wait_send())
    for q in hops:
        pl.when(q < hop_up)(lambda: hop_copy(True, q).wait_send())
        pl.when(q < hop_down)(lambda: hop_copy(False, q).wait_send())
        pl.when(q < pass_up)(lambda: pass_copy(True, q).wait_send())
        pl.when(q < pass_down)(lambda: pass_copy(False, q).wait_send())
    for k in range(2):
        pl.when(has_high)(lambda: rad_copy(True, k).wait_send())
        pl.when(has_low)(lambda: rad_copy(False, k).wait_send())


def write_kernel(ns, nst, out_state, out_section, sem):
    copies = []
    for c in range(ns.shape[1]):
        copies.append(pltpu.make_async_copy(ns.at[:, c], out_section.at[:, c], sem.at[0, c]))
        copies.append(pltpu.make_async_copy(nst.at[:, c], out_state.at[:, c], sem.at[1, c]))
    for copy in copies:
        copy.start()
    for copy in copies:
        copy.wait()


def body(mesh_sizes, state, section, mean_axial, mean_swirl, mean_density, sound_squared):
    n_ax, n_az, n_rad = mesh_sizes
    _, count, rows, local = state.shape
    near_t = jnp.asarray(near_table(local))
    into_t, outof_t = (jnp.asarray(table) for table in far_tables(n_az, local))
    whole = (5, count, rows, local)
    far = pl.BlockSpec(memory_space=pltpu.HBM)
    near = pl.BlockSpec(memory_space=pltpu.VMEM)
    f32 = jnp.float32
    dma = pltpu.SemaphoreType.DMA
    pin = functools.partial(pltpu.with_memory_space_constraint, memory_space=pltpu.HBM)
    cut = rows // CUTS
    ns, nst = pl.pallas_call(
        functools.partial(kernel, (n_ax, n_az, n_rad, count, rows, local)),
        out_shape=tuple(pltpu.VMEM(shape, f32) for shape in (whole, whole)),
        in_specs=[far] * 9,
        out_specs=(near,) * 2,
        scratch_shapes=[
            pltpu.VMEM((5, count + 2 * HALO, rows, local), f32),
            pltpu.VMEM((2, count, rows + 2 * RIM, local), f32),
            pltpu.VMEM((2, 5, HALO, rows, local), f32),
            pltpu.VMEM((CUTS - 1, 5, HALO, cut, local), f32),
            pltpu.VMEM((5, count, rows, WIDTH), f32),
            pltpu.VMEM((n_az - 1, 5, count, rows, WIDTH), f32),
            pltpu.VMEM((2, local, local), jnp.bfloat16),
            pltpu.VMEM((2, local, WIDTH), jnp.bfloat16),
            pltpu.VMEM((n_az - 1, 2, WIDTH, local), jnp.bfloat16),
            pltpu.VMEM((8, rows, local), f32),
            pltpu.VMEM((4, 1, rows), f32),
            dma((11,)),
            dma((n_az - 1, count)),
            dma((n_az - 1, count)),
            dma((2, CUTS)),
            dma((2, CUTS)),
            dma((CUTS - 1,)),
            dma((CUTS - 1,)),
            dma((CUTS - 1,)),
            dma((2, 2)),
            dma((2, 2)),
        ],
        compiler_params=pltpu.CompilerParams(
            collective_id=0, has_side_effects=True, vmem_limit_bytes=36 * 2**20
        ),
        cost_estimate=pl.CostEstimate(
            flops=6 * 5 * count * rows * local * NT,
            bytes_accessed=4 * 4 * 5 * count * rows * local,
            transcendentals=0,
        ),
    )(
        pin(state),
        pin(section),
        pin(mean_axial[None]),
        pin(mean_swirl[None]),
        pin(mean_density[None]),
        pin(sound_squared[None]),
        pin(near_t),
        pin(into_t),
        pin(outof_t),
    )
    return pl.pallas_call(
        write_kernel,
        out_shape=(jax.ShapeDtypeStruct(whole, f32), jax.ShapeDtypeStruct(whole, f32)),
        in_specs=[near] * 2,
        out_specs=(far, far),
        scratch_shapes=[dma((2, count))],
        compiler_params=pltpu.CompilerParams(vmem_limit_bytes=4 * 2**20),
    )(ns, nst)


def solution(mesh):
    spec = P(None, "ax", "rad", "az")
    sizes = (mesh.shape["ax"], mesh.shape["az"], mesh.shape["rad"])
    return jax.shard_map(
        functools.partial(body, sizes),
        mesh=mesh,
        in_specs=(spec, spec, P("rad"), P("rad"), P("rad"), P("rad")),
        out_specs=(spec, spec),
        check_vma=False,
    )
```

time: 123 us -> 84.6 us (0.69)
  Pallas kernels: 122 us -> 83.8 us
    pallas_call x1, Pallas kernels: 118 us -> 79.7 us  [body(): pl.pallas_call(functools.partial(kernel, (n_ax, n_az, n_rad, count, rows,...]
where the time goes in v1:
time: 84.6 us; the launch traced here: 84.4 us
  Pallas kernels  83.8 us (99%)
    pallas_call x1, Pallas kernels, body(): pl.pallas_call(functools.partial(kernel, (n_ax, n_az, n_rad, count, rows,...  79.7 us
    pallas_call x1, Pallas kernels, body(): pl.pallas_call(write_kernel, out_shape=(jax.ShapeDtypeStruct(whole, f32),...  4.06 us

profile of v1, /device:TPU:0, one launch (start us, length us, event | category | flops | bytes accessed | tf_op | source)
XLA Modules:
  0.0 84.4 jit_solution(14179166792869704282)
XLA Ops:
  0.6 79.7 %shard_map.104 = (f32[5,8,64,512]{3,2,1,0:T(8,128)S(1)}, f32[5,8,64,512]{3,2,1,0:T(8,128)S(1)}) custom-call(f32[5,8,64,512]{3,2,1,0:T(8,128)} %state.1, f32[5,8,64,512]{3,2,1,0:T(8,128)} %section.1, f32[1,64]{1,0:T(1,128)} %bitcast.4, f32[1,64]{1,0:T(1,128)} %bitcast.5, f32[1,64]{1,0:T(1,128)} %bitcast.6, f32[1,64]{1,0:T(1,128)} %bitcast.7, ...), custom_call_target="tpu_custom_call" | custom-call | flops 8053063680 | bytes 20971520 | tf_op jit(solution)/shard_map/pallas_call | solution.py:409
  80.3 4.1 %shard_map.105 = (f32[5,8,64,512]{3,2,1,0:T(8,128)}, f32[5,8,64,512]{3,2,1,0:T(8,128)}) custom-call(f32[5,8,64,512]{3,2,1,0:T(8,128)S(1)} %get-tuple-element.4.ns, f32[5,8,64,512]{3,2,1,0:T(8,128)S(1)} %get-tuple-element.5.nst), custom_call_target="tpu_custom_call" | custom-call | tf_op jit(solution)/shard_map/pallas_call | solution.py:456

commit v2 on v1

--- a/solution.py
+++ b/solution.py
@@ -72,9 +72,27 @@
     return dot(high, high_table) + dot(low, high_table) + dot(high, low_table)
 
 
+def rim_terms(halo, way, lines, coef, rows, reach):
+    grads = []
+    for f in range(5):
+        total = 0.0
+        for j in range(reach + 1, HALO + 1):
+            past = j - reach - 1
+            total += drp_coeffs[j - 1] * halo[way, f, past if way else HALO - 1 - past, lines]
+        grads.append(total if way else -total)
+    speed, dense, stiff, inverse = coef[0, rows], coef[2, rows], coef[3, rows], coef[4, rows]
+    return (
+        speed * grads[0] + dense * grads[1],
+        speed * grads[1] + inverse * grads[4],
+        speed * grads[2],
+        speed * grads[3],
+        speed * grads[4] + stiff * grads[1],
+    )
+
+
 def kernel(
-    sizes, state, section, axial_speed, swirl, density_in, sound, near_in, into_in, outof_in, ns, nst,
-    st, pr, halo, relay, sums, other, near, into, outof, coef, means,
+    sizes, state, section, axial_speed, swirl, density_in, sound, near_in, into_in, outof_in, ns, nst, late, coef,
+    st, pr, halo, relay, sums, other, near, into, outof, means,
     load_sem, az_send, az_recv, ax_send, ax_recv, hop_send, hop_recv, pass_send, rad_send, rad_recv,
 ):
     n_ax, n_az, n_rad, count, rows, local = sizes
@@ -115,7 +133,8 @@
         return state.at[:, pl.ds(count - HALO if up else 0, HALO), pl.ds(q * cut, cut)]
 
     def landing(up, q):
-        return halo.at[0 if up else 1, :, :, pl.ds(q * cut, cut)]
+        way = 0 if up else 1
+        return late.at[way] if q == CUTS - 1 else halo.at[way, :, :, pl.ds(q * cut, cut)]
 
     def ax_copy(up, q):
         way = 0 if up else 1
@@ -187,8 +206,6 @@
     pl.when(has_low)(lambda: greet("rad", rad - 1))
     pl.when(has_high)(lambda: greet("rad", rad + 1))
     met = met + has_low.astype(jnp.int32) + has_high.astype(jnp.int32)
-    for copy in vectors + loads:
-        copy.start()
     pl.semaphore_wait(barrier, met)
 
     up_direct = lambda q: jnp.logical_and(has_next, q >= hop_up)
@@ -210,6 +227,8 @@
         pl.when(has_high)(lambda: rad_copy(True, k).start())
         pl.when(has_low)(lambda: rad_copy(False, k).start())
 
+    for copy in vectors + loads:
+        copy.start()
     for copy in vectors:
         copy.wait()
 
@@ -287,6 +306,11 @@
         for j in range(1, 4):
             total += drp_coeffs[j - 1] * (st[f, c + HALO + j] - st[f, c + HALO - j])
         return total
+
+    for way, there in enumerate((has_prev, has_next)):
+        @pl.when(jnp.logical_not(there))
+        def _():
+            late[way] = jnp.zeros_like(late[way])
 
     def pass_on(q):
         @pl.when(q < pass_up)
@@ -329,31 +353,16 @@
     lax.fori_loop(0, count, plane, 0)
 
     def rim(up, q):
-        way = 0 if up else 1
         lines = pl.ds(q * cut, cut)
-        speed, dense, stiff, inverse = coef[0, lines], coef[2, lines], coef[3, lines], coef[4, lines]
         for reach in range(HALO):
             p = reach if up else count - 1 - reach
-            grads = []
-            for f in range(5):
-                total = jnp.zeros((cut, local), jnp.float32)
-                for j in range(reach + 1, HALO + 1):
-                    past = j - reach - 1
-                    total += drp_coeffs[j - 1] * halo[way, f, HALO - 1 - past if up else past, lines]
-                grads.append(-total if up else total)
-            more = (
-                speed * grads[0] + dense * grads[1],
-                speed * grads[1] + inverse * grads[4],
-                speed * grads[2],
-                speed * grads[3],
-                speed * grads[4] + stiff * grads[1],
-            )
+            more = rim_terms(halo, 0 if up else 1, lines, coef, lines, reach)
             for f in range(5):
                 value = ns[f, p, lines] + more[f]
                 ns[f, p, lines] = value
                 nst[f, p, lines] = st[f, HALO + p, lines] + section_gain * value
 
-    for q in range(CUTS):
+    for q in range(CUTS - 1):
         @pl.when(has_prev)
         def _():
             ax_copy(True, q).wait_recv()
@@ -381,15 +390,40 @@
     for k in range(2):
         pl.when(has_high)(lambda: rad_copy(True, k).wait_send())
         pl.when(has_low)(lambda: rad_copy(False, k).wait_send())
-
-
-def write_kernel(ns, nst, out_state, out_section, sem):
+    pl.when(has_prev)(lambda: ax_copy(True, CUTS - 1).wait_recv())
+    pl.when(has_next)(lambda: ax_copy(False, CUTS - 1).wait_recv())
+
+
+def write_kernel(ns, nst, late, coef, out_state, out_section, fin, sem, last_sem):
+    _, count, rows, _ = ns.shape
+    cut = rows // CUTS
+    done = rows - cut
+    ends = pl.ds(done, cut)
+    rims = sorted({*range(min(HALO, count)), *range(max(count - HALO, 0), count)})
+    pairs = ((ns, out_section), (nst, out_state))
     copies = []
-    for c in range(ns.shape[1]):
-        copies.append(pltpu.make_async_copy(ns.at[:, c], out_section.at[:, c], sem.at[0, c]))
-        copies.append(pltpu.make_async_copy(nst.at[:, c], out_state.at[:, c], sem.at[1, c]))
+    for c in range(count):
+        lines = pl.ds(0, done if c in rims else rows)
+        for i, (source, target) in enumerate(pairs):
+            copies.append(
+                pltpu.make_async_copy(source.at[:, c, lines], target.at[:, c, lines], sem.at[i, c])
+            )
     for copy in copies:
         copy.start()
+    for slot, p in enumerate(rims):
+        more = [0.0] * 5
+        if p < HALO:
+            more = [a + b for a, b in zip(more, rim_terms(late, 0, slice(None), coef, ends, p))]
+        if p >= count - HALO:
+            more = [a + b for a, b in zip(more, rim_terms(late, 1, slice(None), coef, ends, count - 1 - p))]
+        for f in range(5):
+            fin[0, f, slot] = ns[f, p, ends] + more[f]
+            fin[1, f, slot] = nst[f, p, ends] + section_gain * more[f]
+        for i, (_, target) in enumerate(pairs):
+            copies.append(
+                pltpu.make_async_copy(fin.at[i, :, slot], target.at[:, p, ends], last_sem.at[i, slot])
+            )
+            copies[-1].start()
     for copy in copies:
         copy.wait()
 
@@ -406,22 +440,22 @@
     dma = pltpu.SemaphoreType.DMA
     pin = functools.partial(pltpu.with_memory_space_constraint, memory_space=pltpu.HBM)
     cut = rows // CUTS
-    ns, nst = pl.pallas_call(
+    edge = (2, 5, HALO, cut, local)
+    ns, nst, late, coef = pl.pallas_call(
         functools.partial(kernel, (n_ax, n_az, n_rad, count, rows, local)),
-        out_shape=tuple(pltpu.VMEM(shape, f32) for shape in (whole, whole)),
+        out_shape=tuple(pltpu.VMEM(shape, f32) for shape in (whole, whole, edge, (8, rows, local))),
         in_specs=[far] * 9,
-        out_specs=(near,) * 2,
+        out_specs=(near,) * 4,
         scratch_shapes=[
             pltpu.VMEM((5, count + 2 * HALO, rows, local), f32),
             pltpu.VMEM((2, count, rows + 2 * RIM, local), f32),
-            pltpu.VMEM((2, 5, HALO, rows, local), f32),
+            pltpu.VMEM((2, 5, HALO, rows - cut, local), f32),
             pltpu.VMEM((CUTS - 1, 5, HALO, cut, local), f32),
             pltpu.VMEM((5, count, rows, WIDTH), f32),
             pltpu.VMEM((n_az - 1, 5, count, rows, WIDTH), f32),
             pltpu.VMEM((2, local, local), jnp.bfloat16),
             pltpu.VMEM((2, local, WIDTH), jnp.bfloat16),
             pltpu.VMEM((n_az - 1, 2, WIDTH, local), jnp.bfloat16),
-            pltpu.VMEM((8, rows, local), f32),
             pltpu.VMEM((4, 1, rows), f32),
             dma((11,)),
             dma((n_az - 1, count)),
@@ -456,11 +490,15 @@
     return pl.pallas_call(
         write_kernel,
         out_shape=(jax.ShapeDtypeStruct(whole, f32), jax.ShapeDtypeStruct(whole, f32)),
-        in_specs=[near] * 2,
+        in_specs=[near] * 4,
         out_specs=(far, far),
-        scratch_shapes=[dma((2, count))],
+        scratch_shapes=[
+            pltpu.VMEM((2, 5, min(2 * HALO, count), cut, local), f32),
+            dma((2, count)),
+            dma((2, min(2 * HALO, count))),
+        ],
         compiler_params=pltpu.CompilerParams(vmem_limit_bytes=4 * 2**20),
-    )(ns, nst)
+    )(ns, nst, late, coef)
 
 
 def solution(mesh):

time: 84.6 us -> 84.4 us (level)
  no operation moved by 1% of the time
where the time goes in v2:
time: 84.4 us; the launch traced here: 84.2 us
  Pallas kernels  83.6 us (99%)
    pallas_call x1, Pallas kernels, body(): pl.pallas_call(functools.partial(kernel, (n_ax, n_az, n_rad, count, rows,...  79.5 us
    pallas_call x1, Pallas kernels, body(): pl.pallas_call(write_kernel, out_shape=(jax.ShapeDtypeStruct(whole, f32),...  4.14 us

profile of v2, /device:TPU:0, one launch (start us, length us, event | category | flops | bytes accessed | tf_op | source)
XLA Modules:
  0.0 84.2 jit_solution(13591481616685079606)
XLA Ops:
  0.6 79.5 %shard_map.104 = (f32[5,8,64,512]{3,2,1,0:T(8,128)S(1)}, f32[5,8,64,512]{3,2,1,0:T(8,128)S(1)}, f32[2,5,3,16,512]{4,3,2,1,0:T(8,128)S(1)}, f32[8,64,512]{2,1,0:T(8,128)S(1)}) custom-call(f32[5,8,64,512]{3,2,1,0:T(8,128)} %state.1, f32[5,8,64,512]{3,2,1,0:T(8,128)} %section.1, f32[1,64]{1,0:T(1,128)} %bitcast.4, f32[1,64]{1,0:T(1,128)} %bitcast.5, ...), custom_call_target="tpu_custom_call" | custom-call | flops 8053063680 | bytes 20971520 | tf_op jit(solution)/shard_map/pallas_call | solution.py:444
  80.1 4.1 %shard_map.105 = (f32[5,8,64,512]{3,2,1,0:T(8,128)}, f32[5,8,64,512]{3,2,1,0:T(8,128)}) custom-call(f32[5,8,64,512]{3,2,1,0:T(8,128)S(1)} %get-tuple-element.6.ns, f32[5,8,64,512]{3,2,1,0:T(8,128)S(1)} %get-tuple-element.7.nst, f32[2,5,3,16,512]{4,3,2,1,0:T(8,128)S(1)} %get-tuple-element.8.late, f32[8,64,512]{2,1,0:T(8,128)S(1)} %get-tuple-element.9.coef), custom_call_target="tpu_custom_call" | custom-call | tf_op jit(solution)/shard_map/pallas_call | solution.py:490

commit v3 on v2

--- a/solution.py
+++ b/solution.py
@@ -119,12 +119,15 @@
         hop_up = hop_down = pass_up = pass_down = zero
     hops = range(CUTS - 1 if levels else 0)
 
-    def az_copy(d, c):
+    half = count // 2
+
+    def az_copy(d, g):
+        planes = pl.ds(g * half, half if g == 0 else count - half)
         return pltpu.make_async_remote_copy(
-            src_ref=sums.at[:, c],
-            dst_ref=other.at[d - 1, :, c],
-            send_sem=az_send.at[d - 1, c],
-            recv_sem=az_recv.at[d - 1, c],
+            src_ref=sums.at[:, planes],
+            dst_ref=other.at[d - 1, :, planes],
+            send_sem=az_send.at[d - 1, g],
+            recv_sem=az_recv.at[d - 1, g],
             device_id={"az": lax.rem(az + d, n_az)},
             device_id_type=MESH,
         )
@@ -261,11 +264,12 @@
     def gather(c, carry):
         flat = st[:, HALO + c].reshape(5 * rows, local)
         sums[:, c] = product(flat, into[0], into[1]).reshape(5, rows, WIDTH)
+        return carry
+
+    for g, (start, stop) in enumerate(((0, half), (half, count))):
+        lax.fori_loop(start, stop, gather, 0)
         for d in range(1, n_az):
-            az_copy(d, c).start()
-        return carry
-
-    lax.fori_loop(0, count, gather, 0)
+            az_copy(d, g).start()
 
     for start in (0, count + HALO):
         st[:, pl.ds(start, HALO)] = jnp.zeros((5, HALO, rows, local), jnp.float32)
@@ -333,9 +337,18 @@
         ns[2, c] = section_keep * ns[2, c] + speed * axial(2, c) + coef[4] * radial(1, c)
         ns[3, c] = section_keep * ns[3, c] + speed * axial(3, c)
         ns[4, c] = section_keep * ns[4, c] + speed * press + coef[3] * (along + spread)
+        @pl.when(c == 0)
+        def _():
+            for d in range(1, n_az):
+                az_copy(d, 0).wait_recv()
+
+        @pl.when(c == half)
+        def _():
+            for d in range(1, n_az):
+                az_copy(d, 1).wait_recv()
+
         g = product(st[:, HALO + c].reshape(5 * rows, local), near[0], near[1])
         for d in range(1, n_az):
-            az_copy(d, c).wait_recv()
             g += product(other[d - 1, :, c].reshape(5 * rows, WIDTH), outof[d - 1, 0], outof[d - 1, 1])
         g = g.reshape(5, rows, local)
         rate = coef[1]
@@ -373,12 +386,9 @@
             ax_copy(False, q).wait_recv()
             rim(False, q)
 
-    def drain(c, carry):
-        for d in range(1, n_az):
-            az_copy(d, c).wait_send()
-        return carry
-
-    lax.fori_loop(0, count, drain, 0)
+    for d in range(1, n_az):
+        for g in range(2):
+            az_copy(d, g).wait_send()
     for q in range(CUTS):
         pl.when(up_direct(q))(lambda: ax_copy(True, q).wait_send())
         pl.when(down_direct(q))(lambda: ax_copy(False, q).wait_send())
@@ -458,8 +468,8 @@
             pltpu.VMEM((n_az - 1, 2, WIDTH, local), jnp.bfloat16),
             pltpu.VMEM((4, 1, rows), f32),
             dma((11,)),
-            dma((n_az - 1, count)),
-            dma((n_az - 1, count)),
+            dma((n_az - 1, 2)),
+            dma((n_az - 1, 2)),
             dma((2, CUTS)),
             dma((2, CUTS)),
             dma((CUTS - 1,)),

time: 84.4 us -> 84.3 us (level)
  no operation moved by 1% of the time
where the time goes in v3:
time: 84.3 us; the launch traced here: 84.1 us
  Pallas kernels  83.5 us (99%)
    pallas_call x1, Pallas kernels, body(): pl.pallas_call(functools.partial(kernel, (n_ax, n_az, n_rad, count, rows,...  79.4 us
    pallas_call x1, Pallas kernels, body(): pl.pallas_call(write_kernel, out_shape=(jax.ShapeDtypeStruct(whole, f32),...  4.14 us

profile of v3, /device:TPU:0, one launch (start us, length us, event | category | flops | bytes accessed | tf_op | source)
XLA Modules:
  0.0 84.1 jit_solution(559900582776438271)
XLA Ops:
  0.6 79.4 %shard_map.104 = (f32[5,8,64,512]{3,2,1,0:T(8,128)S(1)}, f32[5,8,64,512]{3,2,1,0:T(8,128)S(1)}, f32[2,5,3,16,512]{4,3,2,1,0:T(8,128)S(1)}, f32[8,64,512]{2,1,0:T(8,128)S(1)}) custom-call(f32[5,8,64,512]{3,2,1,0:T(8,128)} %state.1, f32[5,8,64,512]{3,2,1,0:T(8,128)} %section.1, f32[1,64]{1,0:T(1,128)} %bitcast.4, f32[1,64]{1,0:T(1,128)} %bitcast.5, ...), custom_call_target="tpu_custom_call" | custom-call | flops 8053063680 | bytes 20971520 | tf_op jit(solution)/shard_map/pallas_call | solution.py:454
  80.0 4.1 %shard_map.105 = (f32[5,8,64,512]{3,2,1,0:T(8,128)}, f32[5,8,64,512]{3,2,1,0:T(8,128)}) custom-call(f32[5,8,64,512]{3,2,1,0:T(8,128)S(1)} %get-tuple-element.6.ns, f32[5,8,64,512]{3,2,1,0:T(8,128)S(1)} %get-tuple-element.7.nst, f32[2,5,3,16,512]{4,3,2,1,0:T(8,128)S(1)} %get-tuple-element.8.late, f32[8,64,512]{2,1,0:T(8,128)S(1)} %get-tuple-element.9.coef), custom_call_target="tpu_custom_call" | custom-call | tf_op jit(solution)/shard_map/pallas_call | solution.py:500

commit v4 on v3

--- a/solution.py
+++ b/solution.py
@@ -230,7 +230,7 @@
         pl.when(has_high)(lambda: rad_copy(True, k).start())
         pl.when(has_low)(lambda: rad_copy(False, k).start())
 
-    for copy in vectors + loads:
+    for copy in vectors + loads[:2]:
         copy.start()
     for copy in vectors:
         copy.wait()
@@ -270,6 +270,9 @@
         lax.fori_loop(start, stop, gather, 0)
         for d in range(1, n_az):
             az_copy(d, g).start()
+
+    for copy in loads[2:]:
+        copy.start()
 
     for start in (0, count + HALO):
         st[:, pl.ds(start, HALO)] = jnp.zeros((5, HALO, rows, local), jnp.float32)

time: 84.3 us -> 84.3 us (level)
  no operation moved by 1% of the time
where the time goes in v4:
time: 84.3 us; the launch traced here: 84.1 us
  Pallas kernels  83.5 us (99%)
    pallas_call x1, Pallas kernels, body(): pl.pallas_call(functools.partial(kernel, (n_ax, n_az, n_rad, count, rows,...  79.4 us
    pallas_call x1, Pallas kernels, body(): pl.pallas_call(write_kernel, out_shape=(jax.ShapeDtypeStruct(whole, f32),...  4.14 us

profile of v4, /device:TPU:0, one launch (start us, length us, event | category | flops | bytes accessed | tf_op | source)
XLA Modules:
  0.0 84.1 jit_solution(11633502312525643551)
XLA Ops:
  0.6 79.4 %shard_map.104 = (f32[5,8,64,512]{3,2,1,0:T(8,128)S(1)}, f32[5,8,64,512]{3,2,1,0:T(8,128)S(1)}, f32[2,5,3,16,512]{4,3,2,1,0:T(8,128)S(1)}, f32[8,64,512]{2,1,0:T(8,128)S(1)}) custom-call(f32[5,8,64,512]{3,2,1,0:T(8,128)} %state.1, f32[5,8,64,512]{3,2,1,0:T(8,128)} %section.1, f32[1,64]{1,0:T(1,128)} %bitcast.4, f32[1,64]{1,0:T(1,128)} %bitcast.5, ...), custom_call_target="tpu_custom_call" | custom-call | flops 8053063680 | bytes 20971520 | tf_op jit(solution)/shard_map/pallas_call | solution.py:457
  80.0 4.1 %shard_map.105 = (f32[5,8,64,512]{3,2,1,0:T(8,128)}, f32[5,8,64,512]{3,2,1,0:T(8,128)}) custom-call(f32[5,8,64,512]{3,2,1,0:T(8,128)S(1)} %get-tuple-element.6.ns, f32[5,8,64,512]{3,2,1,0:T(8,128)S(1)} %get-tuple-element.7.nst, f32[2,5,3,16,512]{4,3,2,1,0:T(8,128)S(1)} %get-tuple-element.8.late, f32[8,64,512]{2,1,0:T(8,128)S(1)} %get-tuple-element.9.coef), custom_call_target="tpu_custom_call" | custom-call | tf_op jit(solution)/shard_map/pallas_call | solution.py:503
